TPU v7x, 512 devices: a whole 4x4x16 slice. The times are simulated.
512 devices in a mesh: seq: 128 (over z, x, core), mp: 4 (over y).
Axes of the slice: x: 4, y: 4, z: 16, core: 2. Of those that a mesh axis runs over, the one named last changes fastest.
Arguments:
- queries: bfloat16 [16384, 4096], P(('seq', 'mp')), may hold values from -120 to 120
- keys: bfloat16 [16384, 4096], P(('seq', 'mp')), may hold values from -6 to 6
- values: bfloat16 [16384, 4096], P(('seq', 'mp')), may hold values from -6 to 6
- text_queries: bfloat16 [16384, 4096], P(('seq', 'mp')), may hold values from -6 to 6
- text_states: bfloat16 [2, 128, 300, 4096], P(None, 'seq', None, 'mp'), may hold values from -6 to 6
- packed_pos: int32 [16384], P('seq'), may hold values from 0 to 16383, as said below
- image_of: int32 [16384], P('seq'), may hold values from 0 to 127, as said below
Outputs:
- attended: bfloat16 [16384, 4096], P('seq', 'mp')
Inputs may be any that keep to these rules, and one draw needn't show every extreme that they name: packed_pos is a permutation; the rows that one index of seq holds send exactly 128 // 128 rows to the packed rows of each index of seq (packed rows k * 128 to (k+1) * 128 - 1 belong to index k). `image_of`: ids never fall along the rows and every image has rows; the rows of image i lie within the packed rows of the seq indices i and i + 1.
All inputs are finite; a program needn't handle non-finite values.
Results may differ from a plain program's by a relative error of at most 0.0049.
Values may be sent and summed in bfloat16 or wider, within the bound.
A program may use at most 64 MiB of HBM per device.

v0:
```python
import math

import jax
import jax.numpy as jnp
from jax import lax
from jax.sharding import PartitionSpec as P

HD = 128


def extended(shard, sides, width):
    for axis, dim in sides:
        size, length = (lax.axis_size(axis), shard.shape[dim])
        up = [(i, (i + 1) % size) for i in range(size - 1)]
        down = [(j, i) for i, j in up]
        last = lax.slice_in_dim(shard, length - width, length, axis=dim)
        first = lax.slice_in_dim(shard, 0, width, axis=dim)
        before = lax.ppermute(last, axis, up)
        after = lax.ppermute(first, axis, down)
        shard = jnp.concatenate([before, shard, after], axis=dim)
    return shard


def passed_along(value, axis, steps):
    count = lax.axis_size(axis)
    first, last = (max(0, -steps), min(count, count - steps))
    return lax.ppermute(value, axis, [(source, source + steps) for source in range(first, last)])


def attend(query, key_rows, value_rows, mask):
    scale = 1.0 / math.sqrt(query.shape[2])
    scores = jnp.einsum("qhd,khd->hqk", query, key_rows, preferred_element_type=jnp.float32) * scale
    scores = jnp.where(mask[None], scores, -1e30)
    top = jnp.max(scores, axis=2, keepdims=True)
    expo = jnp.exp(scores - top)
    weights = (expo / jnp.sum(expo, axis=2, keepdims=True)).astype(jnp.bfloat16)
    return jnp.einsum("hqk,khd->qhd", weights, value_rows, preferred_element_type=jnp.float32)


def body(queries, keys, values, text_queries, text_states, packed_pos, image_of):
    stacked = jnp.stack([queries, keys, values, text_queries])
    split = lax.all_to_all(stacked, "mp", split_axis=2, concat_axis=1, tiled=True)
    rows = split.shape[1]
    width = split.shape[2]
    heads = width // HD
    peers = lax.axis_size("seq")
    capacity = rows // peers
    me = lax.axis_index("seq")
    target = packed_pos // rows
    order = jnp.argsort(target, stable=True)
    outgoing = jnp.take(split, order, axis=1).reshape(4, peers, capacity, width)
    slots = (packed_pos % rows)[order].reshape(1, peers, capacity)
    incoming, landing = (
        lax.all_to_all(outgoing, "seq", split_axis=1, concat_axis=1, tiled=True),
        lax.all_to_all(slots, "seq", split_axis=1, concat_axis=1, tiled=True),
    )
    placing = jnp.argsort(landing.reshape(rows))
    packed = jnp.take(incoming.reshape(4, rows, width), placing, axis=1)
    shaped = packed.reshape(4, rows, heads, HD)
    own_ids = (image_of + 1).reshape(1, rows)
    nearby, near_ids = (
        extended(packed[1:3], (("seq", 1),), rows),
        extended(own_ids, (("seq", 1),), rows),
    )
    self_mask = own_ids[0][:, None] == near_ids[0][None, :]
    nearby = nearby.reshape(2, 3 * rows, heads, HD)
    self_out = attend(shaped[0], nearby[0], nearby[1], self_mask)
    prompts = text_states.shape[1]
    length = text_states.shape[2]
    earlier = passed_along(text_states, "seq", 1)
    chosen = jnp.concatenate([earlier, text_states], axis=1).reshape(
        2, 2 * prompts * length, heads, HD
    )
    chosen_ids = (me - 1) * prompts + jnp.arange(2 * prompts * length, dtype=jnp.int32) // length
    cross_mask = image_of[:, None] == chosen_ids[None, :]
    cross_out = attend(shaped[3], chosen[0], chosen[1], cross_mask)
    return (self_out + cross_out).reshape(rows, width).astype(jnp.bfloat16)


def solution(mesh):
    return jax.shard_map(
        body,
        mesh=mesh,
        in_specs=(
            P(("seq", "mp"), None),
            P(("seq", "mp"), None),
            P(("seq", "mp"), None),
            P(("seq", "mp"), None),
            P(None, "seq", None, "mp"),
            P("seq"),
            P("seq"),
        ),
        out_specs=P("seq", "mp"),
        check_vma=False,
    )
```

profile of v0, /device:TPU:103, one launch (start us, length us, event | category | flops | bytes accessed | tf_op | source)
XLA Modules:
  0.0 209.5 jit_solution(13007391793037084214)
XLA Ops:
  0.0 1.3 pad_maximum_fusion.1
  1.3 4.7 %copy.52 = bf16[4,32,4096]{1,0,2:T(4,128)(2,1)} copy(bf16[4,32,4096]{2,1,0:T(8,128)(2,1)S(1)} %pad_maximum_fusion.1) | data formatting | bytes 2097152 | tf_op jit(solution)/shard_map/stack | solution.py:41
  6.0 6.4 %reshape.149 = bf16[4,2,65536]{2,1,0:T(2,128)(2,1)} reshape(bf16[4096,4,32]{2,1,0:T(4,128)(2,1)} %bitcast.38) | data formatting | bytes 2097152
  12.4 4.3 %all-to-all-start = ((bf16[4,2,65536]{2,1,0:T(2,128)(2,1)}), bf16[4,2,65536]{2,1,0:T(2,128)(2,1)S(1)}, u32[]{:S(2)}, u32[]{:S(2)}) async-start(bf16[4,2,65536]{2,1,0:T(2,128)(2,1)} %reshape.149), calls=%async_computation | async-start | bytes 2097152 | tf_op jit(solution)/shard_map/all_to_all | solution.py:42
  16.7 0.0 copy-done.8
  16.8 2.5 %sort.34 = (s32[128]{0:T(128)}, s32[128]{0:T(128)S(1)}) sort(s32[128]{0:T(128)S(1)} %get-tuple-element.19, s32[128]{0:T(128)S(1)} %iota.13), dimensions={0}, to_apply=%region_0.1 | sort | flops 896 | bytes 2048 | tf_op jit(solution)/shard_map/jit(argsort)/sort | solution.py:50
  19.3 1.2 gather_fusion
  20.5 0.7 copy.51
  21.3 9.6 %all-to-all-done = bf16[4,2,65536]{2,1,0:T(2,128)(2,1)S(1)} async-done(((bf16[4,2,65536]{2,1,0:T(2,128)(2,1)}), bf16[4,2,65536]{2,1,0:T(2,128)(2,1)S(1)}, u32[]{:S(2)}, u32[]{:S(2)}) %all-to-all-start) | async-done | bytes 1048608 | tf_op jit(solution)/shard_map/all_to_all | solution.py:42
  30.9 19.6 %all-to-all-start.2 = ((s32[1,128,1]{2,0,1:T(1,128)}), s32[1,128,1]{2,0,1:T(1,128)S(1)}, u32[]{:S(2)}, u32[]{:S(2)}) async-start(s32[1,128,1]{2,0,1:T(1,128)} %copy.51), calls=%async_computation.2 | async-start | bytes 131072 | tf_op jit(solution)/shard_map/all_to_all | solution.py:55
  50.5 3.5 %reshape.150 = bf16[4096,4,32]{2,1,0:T(4,128)(2,1)} reshape(bf16[4,2,65536]{2,1,0:T(2,128)(2,1)S(1)} %all-to-all-done) | data formatting | bytes 2097152
  54.1 5.5 %copy.54 = bf16[4,4,32,1024]{3,2,1,0:T(8,128)(2,1)S(1)} copy(bf16[4,4,32,1024]{2,0,3,1:T(4,128)(2,1)} %bitcast.39) | data formatting | bytes 2097152 | tf_op jit(solution)/shard_map/all_to_all | solution.py:42
  59.6 0.8 copy.55
  60.4 1.4 gather_fusion.1
  61.9 1.5 select_bitcast_fusion.1
  63.4 0.0 all-to-all-done.2
  63.4 0.6 copy-done.4
  64.0 16.1 %all-to-all-start.1 = ((bf16[4,128,1,1024]{3,0,2,1:T(4,128)(2,1)}), bf16[4,128,1,1024]{3,0,2,1:T(4,128)(2,1)S(1)}, u32[]{:S(2)}, u32[]{:S(2)}) async-start(bf16[4,128,1,1024]{3,0,2,1:T(4,128)(2,1)} %select_bitcast_fusion.1), calls=%async_computation.1 | async-start | bytes 2097152 | tf_op jit(solution)/shard_map/all_to_all | solution.py:54
  80.2 0.0 copy-done.1
  80.2 4.6 %collective-permute-start.4 = (bf16[2,1,300,1024]{3,0,2,1:T(2,128)(2,1)S(1)}, bf16[2,1,300,1024]{3,0,2,1:T(2,128)(2,1)S(1)}, u32[]{:S(2)}, u32[]{:S(2)}) collective-permute-start(bf16[2,1,300,1024]{3,0,2,1:T(2,128)(2,1)S(1)} %copy-done.1), channel_id=1, source_target_pairs={{0,4},{4,8},{8,12},{12,16},{16,20},{20,24},{24,28},{28,32},{32,36}... | collective-permute-start | bytes 3686408 | tf_op jit(solution)/shard_map/ppermute | solution.py:27
  84.7 0.0 copy-done.7
  84.8 2.1 collective-permute-start.2
  86.8 2.5 %collective-permute-start.3 = (s32[1,128]{1,0:T(1,128)S(1)}, s32[1,128]{1,0:T(1,128)S(1)}, u32[]{:S(2)}, u32[]{:S(2)}) collective-permute-start(s32[1,128]{1,0:T(1,128)S(1)} %get-tuple-element.17), channel_id=1, source_target_pairs={{4,0},{8,4},{12,8},{16,12},{20,16},{24,20},{28,24},{32,28},{36,32}... | collective-permute-start | bytes 1544 | tf_op jit(solution)/shard_map/ppermute | solution.py:19
  89.3 0.8 broadcast_compare_fusion
  90.1 48.3 %collective-permute-done.2 = s32[1,128]{1,0:T(1,128)S(1)} collective-permute-done((s32[1,128]{1,0:T(1,128)S(1)}, s32[1,128]{1,0:T(1,128)S(1)}, u32[]{:S(2)}, u32[]{:S(2)}) %collective-permute-start.2) | collective-permute-done | bytes 544 | tf_op jit(solution)/shard_map/ppermute | solution.py:18
  138.3 0.0 collective-permute-done.3
  138.4 0.7 broadcast_compare_fusion.1
  139.1 3.2 %reduce = s32[128]{0:T(128)S(1)} reduce(s32[1,128,1]{2,0,1:T(1,128)} %copy-done.4, s32[]{:T(128)} %constant.54.clone.1), dimensions={0,2}, to_apply=%all_to_all.24.reduce_sub_computation | reduce | bytes 1028 | tf_op jit(solution)/shard_map/all_to_all | solution.py:55
  142.3 2.5 %sort.35 = (s32[128]{0:T(128)}, s32[128]{0:T(128)S(1)}) sort(s32[128]{0:T(128)S(1)} %reduce, s32[128]{0:T(128)S(1)} %iota.14), dimensions={0}, to_apply=%region_1.3 | sort | flops 896 | bytes 2048 | tf_op jit(solution)/shard_map/jit(argsort)/sort | solution.py:57
  144.8 0.0 collective-permute-done.4
  144.8 0.8 constant_dynamic-update-slice_fusion.1
  145.7 0.9 constant_dynamic-update-slice_fusion
  146.6 13.9 %slice_reduce_fusion = (bf16[2,300,1024]{2,1,0:T(8,128)(2,1)S(1)}, bf16[2,300,1024]{2,1,0:T(8,128)(2,1)S(1)}) fusion(bf16[2,2,300,1024]{3,0,2,1:T(2,128)(2,1)S(1)} %constant_dynamic-update-slice_fusion), kind=kLoop, calls=%fused_computation.5 | loop fusion | bytes 4915200 | tf_op jit(solution)/shard_map/slice | solution.py:76
  160.5 1.4 squeeze.23
  162.0 1.4 squeeze.21
  163.3 0.0 all-to-all-done.1
  163.3 1.4 gather_fusion.2
  164.8 0.6 select_bitcast_fusion
  165.4 0.6 slice.40
  166.0 0.0 copy-start.2
  166.0 0.0 copy-start.6
  166.0 7.9 %collective-permute-start = (bf16[2,128,1024]{2,0,1:T(2,128)(2,1)S(1)}, bf16[2,128,1024]{2,0,1:T(2,128)(2,1)}, u32[]{:S(2)}, u32[]{:S(2)}) collective-permute-start(bf16[2,128,1024]{2,0,1:T(2,128)(2,1)S(1)} %slice.40), channel_id=1, source_target_pairs={{0,4},{4,8},{8,12},{12,16},{16,20},{20,24},{24,28},{28,32},{32,36}... | collective-permute-start | bytes 1572872 | tf_op jit(solution)/shard_map/ppermute | solution.py:18
  173.9 2.1 %collective-permute-start.1 = (bf16[2,128,1024]{2,0,1:T(2,128)(2,1)S(1)}, bf16[2,128,1024]{2,0,1:T(2,128)(2,1)}, u32[]{:S(2)}, u32[]{:S(2)}) collective-permute-start(bf16[2,128,1024]{2,0,1:T(2,128)(2,1)S(1)} %slice.40), channel_id=1, source_target_pairs={{4,0},{8,4},{12,8},{16,12},{20,16},{24,20},{28,24},{32,28},{36,32}... | collective-permute-start | bytes 1572872 | tf_op jit(solution)/shard_map/ppermute | solution.py:19
  176.1 0.7 fusion.39
  176.8 0.4 copy.58
  177.3 1.1 copy.62
  178.3 0.0 copy-done.2
  178.3 0.0 copy-done.6
  178.3 2.3 %fusion.40 = f32[8,128]{1,0:T(8,128)S(1)} fusion(pred[128,600]{0,1:T(8,128)(4,1)S(1)} %copy-done.6, bf16[128,8,128]{0,2,1:T(8,128)(2,1)} %bitcast.47, bf16[600,8,128]{2,1,0:T(8,128)(2,1)S(1)} %copy-done.2), kind=kOutput, calls=%fused_computation.64 | convolution fusion | flops 159744592 | bytes 1571840 | tf_op jit(solution)/shard_map/sub | solution.py:35
  180.6 0.0 copy-done.3
  180.6 3.4 %fusion.5 = f32[8,128,128]{2,1,0:T(8,128)} fusion(bf16[600,8,128]{2,1,0:T(8,128)(2,1)S(1)} %copy-done.3, f32[8,128]{1,0:T(8,128)S(1)} %fusion.40, pred[128,600]{0,1:T(8,128)(4,1)S(1)} %copy-done.6, bf16[128,8,128]{0,2,1:T(8,128)(2,1)} %bitcast.48, bf16[600,8,128]{2,1,0:T(8,128)(2,1)S(1)} %copy-done.2), kind=kOutput, calls=%fused_computation.17 | convolution fusion | flops 317646400 | bytes 3324928 | tf_op jit(solution)/shard_map/hqk,khd->qhd/dot_general | solution.py:37
  184.1 0.0 collective-permute-done
  184.1 3.8 %collective-permute-done.1 = bf16[2,128,1024]{2,0,1:T(2,128)(2,1)} collective-permute-done((bf16[2,128,1024]{2,0,1:T(2,128)(2,1)S(1)}, bf16[2,128,1024]{2,0,1:T(2,128)(2,1)}, u32[]{:S(2)}, u32[]{:S(2)}) %collective-permute-start.1) | collective-permute-done | bytes 524320 | tf_op jit(solution)/shard_map/ppermute | solution.py:19
  187.9 6.9 %pad_maximum_fusion = bf16[2,384,1024]{2,0,1:T(2,128)(2,1)S(1)} fusion(bf16[2,128,1024]{2,0,1:T(2,128)(2,1)} %collective-permute-done.1, bf16[2,128,1024]{2,0,1:T(2,128)(2,1)S(1)} %slice.40, bf16[2,128,1024]{2,0,1:T(2,128)(2,1)} %collective-permute-done), kind=kLoop, calls=%fused_computation.12 | loop fusion | flops 1572864 | bytes 3145728 | tf_op jit(solution)/shard_map/concatenate | solution.py:20
  194.7 2.2 %fusion.38 = (bf16[1,384,1024]{2,0,1:T(2,128)(2,1)S(1)}, bf16[1,384,1024]{2,0,1:T(2,128)(2,1)S(1)}) fusion(bf16[2,384,1024]{2,0,1:T(2,128)(2,1)S(1)} %pad_maximum_fusion), kind=kLoop, calls=%fused_computation.62 | loop fusion | bytes 3145728 | tf_op jit(solution)/shard_map/slice | solution.py:67
  197.0 0.0 copy-start.5
  197.0 2.8 %copy.59 = bf16[1,384,1024]{1,2,0:T(8,128)(2,1)} copy(bf16[1,384,1024]{2,0,1:T(2,128)(2,1)S(1)} %get-tuple-element.12) | data formatting | bytes 1572864 | tf_op jit(solution)/shard_map/slice | solution.py:67
  199.8 0.0 copy-done.5
  199.8 2.8 %multiply_select_fusion.2 = f32[8,128,384]{2,1,0:T(8,128)} fusion(bf16[128,8,128]{0,2,1:T(8,128)(2,1)S(1)} %bitcast.44, bf16[384,8,128]{0,2,1:T(8,128)(2,1)} %bitcast.42, pred[128,384]{1,0:T(8,128)(4,1)S(1)} %copy-done.5), kind=kOutput, calls=%fused_computation.14 | convolution fusion | flops 101449728 | bytes 2670592 | tf_op jit(solution)/shard_map/qhd,khd->hqk/dot_general | solution.py:32
  202.6 0.0 copy-done
  202.6 0.8 fusion.43
  203.4 1.3 copy.57
  204.7 3.9 %fusion.12 = bf16[8,128,128]{2,1,0:T(8,128)(2,1)S(1)} fusion(f32[8,128,128]{2,1,0:T(8,128)S(1)} %copy-done.9, bf16[384,8,128]{0,2,1:T(8,128)(2,1)S(1)} %bitcast.46, f32[8,128]{1,0:T(8,128)S(1)} %fusion.43, f32[8,128,384]{2,1,0:T(8,128)} %multiply_select_fusion.2), kind=kOutput, calls=%fused_computation.24 | convolution fusion | flops 102106496 | bytes 3149824 | tf_op jit(solution)/shard_map/hqk,khd->qhd/dot_general | solution.py:37
  208.6 0.9 copy.66
  (20 shorter events, 0.1 us)
Async XLA Ops:
  12.4 4.3 %copy-start.8 = (s32[128]{0:T(128)S(1)}, s32[128]{0:T(128)}, u32[]{:S(2)}) copy-start(s32[128]{0:T(128)} %param.14) | copy-start | bytes 1540
  12.4 18.5 %all-to-all-start = ((bf16[4,2,65536]{2,1,0:T(2,128)(2,1)}), bf16[4,2,65536]{2,1,0:T(2,128)(2,1)S(1)}, u32[]{:S(2)}, u32[]{:S(2)}) async-start(bf16[4,2,65536]{2,1,0:T(2,128)(2,1)} %reshape.149), calls=%async_computation | async-start | bytes 2097152 | tf_op jit(solution)/shard_map/all_to_all | solution.py:42
  30.9 32.5 %all-to-all-start.2 = ((s32[1,128,1]{2,0,1:T(1,128)}), s32[1,128,1]{2,0,1:T(1,128)S(1)}, u32[]{:S(2)}, u32[]{:S(2)}) async-start(s32[1,128,1]{2,0,1:T(1,128)} %copy.51), calls=%async_computation.2 | async-start | bytes 131072 | tf_op jit(solution)/shard_map/all_to_all | solution.py:55
  63.4 16.8 %copy-start.1 = (bf16[2,1,300,1024]{3,0,2,1:T(2,128)(2,1)S(1)}, bf16[2,1,300,1024]{3,0,2,1:T(2,128)(2,1)}, u32[]{:S(2)}) copy-start(bf16[2,1,300,1024]{3,0,2,1:T(2,128)(2,1)} %param.13) | copy-start | bytes 3686404
  63.4 21.3 %copy-start.7 = (s32[128]{0:T(128)S(1)}, s32[128]{0:T(128)}, u32[]{:S(2)}) copy-start(s32[128]{0:T(128)} %param.15) | copy-start | bytes 1540
  63.4 0.6 copy-start.4
  64.0 99.3 %all-to-all-start.1 = ((bf16[4,128,1,1024]{3,0,2,1:T(4,128)(2,1)}), bf16[4,128,1,1024]{3,0,2,1:T(4,128)(2,1)S(1)}, u32[]{:S(2)}, u32[]{:S(2)}) async-start(bf16[4,128,1,1024]{3,0,2,1:T(4,128)(2,1)} %select_bitcast_fusion.1), calls=%async_computation.1 | async-start | bytes 2097152 | tf_op jit(solution)/shard_map/all_to_all | solution.py:54
  80.2 64.7 %collective-permute-start.4 = (bf16[2,1,300,1024]{3,0,2,1:T(2,128)(2,1)S(1)}, bf16[2,1,300,1024]{3,0,2,1:T(2,128)(2,1)S(1)}, u32[]{:S(2)}, u32[]{:S(2)}) collective-permute-start(bf16[2,1,300,1024]{3,0,2,1:T(2,128)(2,1)S(1)} %copy-done.1), channel_id=1, source_target_pairs={{0,4},{4,8},{8,12},{12,16},{16,20},{20,24},{24,28},{28,32},{32,36}... | collective-permute-start | bytes 3686408 | tf_op jit(solution)/shard_map/ppermute | solution.py:27
  84.8 53.6 %collective-permute-start.2 = (s32[1,128]{1,0:T(1,128)S(1)}, s32[1,128]{1,0:T(1,128)S(1)}, u32[]{:S(2)}, u32[]{:S(2)}) collective-permute-start(s32[1,128]{1,0:T(1,128)S(1)} %get-tuple-element.17), channel_id=1, source_target_pairs={{0,4},{4,8},{8,12},{12,16},{16,20},{20,24},{24,28},{28,32},{32,36}... | collective-permute-start | bytes 1544 | tf_op jit(solution)/shard_map/ppermute | solution.py:18
  86.8 51.5 %collective-permute-start.3 = (s32[1,128]{1,0:T(1,128)S(1)}, s32[1,128]{1,0:T(1,128)S(1)}, u32[]{:S(2)}, u32[]{:S(2)}) collective-permute-start(s32[1,128]{1,0:T(1,128)S(1)} %get-tuple-element.17), channel_id=1, source_target_pairs={{4,0},{8,4},{12,8},{16,12},{20,16},{24,20},{28,24},{32,28},{36,32}... | collective-permute-start | bytes 1544 | tf_op jit(solution)/shard_map/ppermute | solution.py:19
  166.0 12.3 %copy-start.2 = (bf16[600,8,128]{2,1,0:T(8,128)(2,1)S(1)}, bf16[600,8,128]{2,1,0:T(8,128)(2,1)}, u32[]{:S(2)}) copy-start(bf16[600,8,128]{2,1,0:T(8,128)(2,1)} %squeeze.23) | copy-start | bytes 3686404
  166.0 12.3 %copy-start.6 = (pred[128,600]{0,1:T(8,128)(4,1)S(1)}, pred[128,600]{0,1:T(8,128)(4,1)}, u32[]{:S(2)}) copy-start(pred[128,600]{0,1:T(8,128)(4,1)} %broadcast_compare_fusion) | copy-start | bytes 230404
  166.0 18.1 %collective-permute-start = (bf16[2,128,1024]{2,0,1:T(2,128)(2,1)S(1)}, bf16[2,128,1024]{2,0,1:T(2,128)(2,1)}, u32[]{:S(2)}, u32[]{:S(2)}) collective-permute-start(bf16[2,128,1024]{2,0,1:T(2,128)(2,1)S(1)} %slice.40), channel_id=1, source_target_pairs={{0,4},{4,8},{8,12},{12,16},{16,20},{20,24},{24,28},{28,32},{32,36}... | collective-permute-start | bytes 1572872 | tf_op jit(solution)/shard_map/ppermute | solution.py:18
  173.9 13.9 %collective-permute-start.1 = (bf16[2,128,1024]{2,0,1:T(2,128)(2,1)S(1)}, bf16[2,128,1024]{2,0,1:T(2,128)(2,1)}, u32[]{:S(2)}, u32[]{:S(2)}) collective-permute-start(bf16[2,128,1024]{2,0,1:T(2,128)(2,1)S(1)} %slice.40), channel_id=1, source_target_pairs={{4,0},{8,4},{12,8},{16,12},{20,16},{24,20},{28,24},{32,28},{36,32}... | collective-permute-start | bytes 1572872 | tf_op jit(solution)/shard_map/ppermute | solution.py:19
  178.3 2.3 %copy-start.3 = (bf16[600,8,128]{2,1,0:T(8,128)(2,1)S(1)}, bf16[600,8,128]{2,1,0:T(8,128)(2,1)}, u32[]{:S(2)}) copy-start(bf16[600,8,128]{2,1,0:T(8,128)(2,1)} %squeeze.21) | copy-start | bytes 3686404
  197.0 2.8 %copy-start.5 = (pred[128,384]{1,0:T(8,128)(4,1)S(1)}, pred[128,384]{1,0:T(8,128)(4,1)}, u32[]{:S(2)}) copy-start(pred[128,384]{1,0:T(8,128)(4,1)} %broadcast_compare_fusion.1) | copy-start | bytes 147460
  199.8 2.8 %copy-start = (bf16[1,384,1024]{1,2,0:T(8,128)(2,1)S(1)}, bf16[1,384,1024]{1,2,0:T(8,128)(2,1)}, u32[]{:S(2)}) copy-start(bf16[1,384,1024]{1,2,0:T(8,128)(2,1)} %copy.59) | copy-start | bytes 2359300
  203.4 1.3 copy-start.9
where the time goes:
time: 210 us; the launch traced here: 209 us
  waiting for transfers between devices  61.7 us (29%)
  starting transfers between devices  59.1 us (28%)
  local copies, waits for them, and re-layouts  55 us (26%)
  other arithmetic  20.2 us (10%)
  matrix products  13.2 us (6%)
    ppermute x2, waiting for transfers between devices, extended(): before = lax.ppermute(last, axis, up)  48.3 us
    all_to_all x1, starting transfers between devices, body(): lax.all_to_all(slots, 'seq', split_axis=1, concat_axis=1, tiled=True)  19.6 us
    all_to_all x1, starting transfers between devices, body(): lax.all_to_all(outgoing, 'seq', split_axis=1, concat_axis=1, tiled=True)  16.1 us
    slice x2, local copies, waits for them, and re-layouts, body(): cross_out = attend(shaped[3], chosen[0], chosen[1], cross_mask)  14.9 us
    unnamed x23, local copies, waits for them, and re-layouts  11.5 us
    ppermute x2, starting transfers between devices, extended(): before = lax.ppermute(last, axis, up)  9.98 us
    all_to_all x1, waiting for transfers between devices, body(): lax.all_to_all(stacked, 'mp', split_axis=2, concat_axis=1, tiled=True)  9.63 us
    slice x5, local copies, waits for them, and re-layouts, body(): self_out = attend(shaped[0], nearby[0], nearby[1], self_mask)  7.54 us
  transfers between devices with their start and end apart: 8, of which 3 were waited for; matrix products, arithmetic and copies ran while one was open for 24% of the time, Pallas kernels for 0%

commit v1 on v0

v1 whole, which is shorter than its diff:
```python
import functools
import math

import jax
import jax.numpy as jnp
from jax import lax
from jax.experimental import pallas as pl
from jax.experimental.pallas import tpu as pltpu
from jax.sharding import PartitionSpec as P

MESH = pl.DeviceIdType.MESH
HD = 128
ROWS = 128
NZ = 16
NW = 8
NY = 4
FEAT = 1024
HEADS = 8
TXT = 300
Q, K, V, T = 0, 1, 2, 3
CHUNKS = ((K, 0, 1024), (V, 0, 1024), (T, 0, 1024), (Q, 0, 512), (Q, 512, 512))
NC = len(CHUNKS)
F32 = jnp.float32
BF16 = jnp.bfloat16
I32 = jnp.int32


def iota(shape, dim):
    return lax.broadcasted_iota(I32, shape, dim)


def one_hot(condition):
    return jnp.where(condition, 1.0, 0.0).astype(BF16)


def dot(a, b):
    return jnp.dot(a, b, preferred_element_type=F32)


def dot_t(a, b):
    return lax.dot_general(a, b, (((1,), (1,)), ((), ())), preferred_element_type=F32)


def kernel(q_ref, k_ref, v_ref, t_ref, text_ref, pos_ref, img_ref, o_ref, *scratch):
    scratch = list(scratch)
    take = lambda n: [scratch.pop(0) for _ in range(n)]
    ybuf, zsend, zrecv, xsend, xrecv = (take(NC) for _ in range(5))
    (packed, kv_prev, kv_next, txt, cross, slot_send, slot_recv, row_send, row_recv, img_near) = take(10)
    (local_sem, y_ssem, y_rsem, z_ssem, z_rsem, x_ssem, x_rsem, n_ssem, n_rsem, t_ssem, t_rsem, s_sems, i_sems) = take(13)
    arrays = (q_ref, k_ref, v_ref, t_ref)

    me = lax.axis_index("seq")
    y = lax.axis_index("mp")
    z, w = me // NW, me % NW
    z_device = lambda other: {"seq": other * NW + w}
    w_device = lambda other: {"seq": z * NW + other}
    after = {"seq": lax.rem(me + 1, NZ * NW)}
    before = {"seq": lax.rem(me + NZ * NW - 1, NZ * NW)}

    def remote(src, dst, send, recv, device):
        return pltpu.make_async_remote_copy(
            src_ref=src, dst_ref=dst, send_sem=send, recv_sem=recv, device_id=device, device_id_type=MESH
        )

    def bytes_of(ref, send, recv):
        return remote(ref, ref, send, recv, after)

    barrier = pltpu.get_barrier_semaphore()
    for i in range(1, NY):
        pl.semaphore_signal(barrier, inc=1, device_id={"mp": lax.rem(y + i, NY)}, device_id_type=MESH)

    def greet_z(i, carry):
        pl.semaphore_signal(barrier, inc=1, device_id=z_device(lax.rem(z + i, NZ)), device_id_type=MESH)
        return carry

    lax.fori_loop(1, NZ, greet_z, 0)

    def greet_w(i, carry):
        pl.semaphore_signal(barrier, inc=1, device_id=w_device(lax.rem(w + i, NW)), device_id_type=MESH)
        return carry

    lax.fori_loop(1, NW, greet_w, 0)
    for device in (after, before):
        pl.semaphore_signal(barrier, inc=1, device_id=device, device_id_type=MESH)

    own = []
    for c, (a, first, columns) in enumerate(CHUNKS):
        start = pl.multiple_of(y * FEAT + first, 128)
        own.append(
            pltpu.make_async_copy(
                arrays[a].at[:, pl.ds(start, columns)], ybuf[c].at[pl.ds(pl.multiple_of(y * 32, 32), 32)], local_sem.at[c]
            )
        )
        own[-1].start()
    own_text = pltpu.make_async_copy(text_ref, txt.at[1], local_sem.at[NC])
    own_text.start()

    pos = pos_ref[...]
    target = lax.shift_right_logical(pos, 7)
    slot = pos & (ROWS - 1)
    image = img_ref[...]
    out_row = iota((2 * ROWS, ROWS), 0)
    same = (lax.shift_right_logical(out_row, 4) * NW + (out_row & 7)) == target
    right_half = (out_row & 8) == 8
    send_left = one_hot(same & ~right_half)
    send_right = one_hot(same & right_half)
    to_z = one_hot(iota((NZ, ROWS), 0) == lax.shift_right_logical(target, 3))
    lane_of = (target & 7) * NZ + z
    by_lane = jnp.where(iota((ROWS, ROWS), 0) == lane_of, slot.astype(F32), 0.0).astype(BF16)
    slots = dot_t(to_z, by_lane).astype(I32)
    for i in range(NZ):
        slot_send[i] = slots[i : i + 1]

    pl.semaphore_wait(barrier, NY - 1 + NZ - 1 + NW - 1 + 2)

    for c, (a, first, columns) in enumerate(CHUNKS):
        for i in range(1, NY):
            other = lax.rem(y + i, NY)
            start = pl.multiple_of(other * FEAT + first, 128)
            remote(
                arrays[a].at[:, pl.ds(start, columns)],
                ybuf[c].at[pl.ds(pl.multiple_of(y * 32, 32), 32)],
                y_ssem.at[c],
                y_rsem.at[c],
                {"mp": other},
            ).start()

    def far_first(i):
        return lax.rem(z + 8 + jnp.where(i % 2 == 0, -(i // 2), i // 2), NZ)

    def send_slots(i, carry):
        to = far_first(i)
        remote(slot_send.at[to], slot_recv.at[z], s_sems.at[0], s_sems.at[1], z_device(to)).start()
        return carry

    lax.fori_loop(1, NZ, send_slots, 0)
    slot_recv[z] = slot_send[z]
    remote(img_ref, img_near.at[0], i_sems.at[0], i_sems.at[1], after).start()
    remote(img_ref, img_near.at[1], i_sems.at[2], i_sems.at[3], before).start()

    for c, (a, first, columns) in enumerate(CHUNKS):
        half = columns // 2
        own[c].wait()
        bytes_of(ybuf[c].at[pl.ds(0, 96)], y_ssem.at[c], y_rsem.at[c]).wait_recv()
        out = dot(send_left, ybuf[c][:, :half]) + dot(send_right, ybuf[c][:, half:])
        zsend[c][...] = out.astype(BF16).reshape(NZ, 16, half)

        def send_z(i, carry):
            to = far_first(i)
            remote(zsend[c].at[to], zrecv[c].at[z], z_ssem.at[c], z_rsem.at[c], z_device(to)).start()
            return carry

        lax.fori_loop(1, NZ, send_z, 0)
        zrecv[c][z] = zsend[c][z]
        if c == 0:
            for i in range(2):
                remote(text_ref.at[i], txt.at[0, i], t_ssem.at[i], t_rsem.at[i], after).start()

    bytes_of(slot_recv.at[pl.ds(0, NZ - 1)], s_sems.at[0], s_sems.at[1]).wait_recv()
    row = slot_recv[0]
    for i in range(1, NZ):
        row = row + slot_recv[i]
    row_send[...] = row

    def send_row(i, carry):
        to = lax.rem(w + i, NW)
        remote(row_send, row_recv.at[w], s_sems.at[2], s_sems.at[3], w_device(to)).start()
        return carry

    lax.fori_loop(1, NW, send_row, 0)
    row_recv[w] = row
    bytes_of(row_recv.at[pl.ds(0, NW - 1)], s_sems.at[2], s_sems.at[3]).wait_recv()
    rows = jnp.concatenate([row_recv[i] for i in range(NW)], axis=0)
    pick = one_hot(iota((ROWS, ROWS), 0) == w * NZ + (iota((ROWS, ROWS), 1) & (NZ - 1)))
    landed = dot(rows.astype(F32).astype(BF16), pick)
    mine = lax.shift_right_logical(iota((NW, ROWS), 1), 4) == iota((NW, ROWS), 0)
    landing = jnp.sum(jnp.where(mine, landed, 0.0), axis=0, keepdims=True).astype(I32)
    place = one_hot(iota((ROWS, ROWS), 0) == landing)

    count = lambda flags: jnp.sum(jnp.where(flags, 1.0, 0.0), axis=1, keepdims=True).astype(I32)
    for i in range(2):
        bytes_of(img_near.at[i], i_sems.at[2 * i], i_sems.at[2 * i + 1]).wait_recv()
    cut = count(image < me)
    cut_prev = count(img_near[0] < me - 1)
    cut_next = count(img_near[1] == me)
    query_row, key_row = iota((ROWS, ROWS), 0), iota((ROWS, ROWS), 1)
    earlier = query_row < cut
    mask_own = earlier == (key_row < cut)
    mask_near = (earlier & (key_row >= cut_prev)) | (~earlier & (key_row < cut_next))
    earlier_text = iota((ROWS, TXT), 0) < cut
    scale = math.log2(math.e) / math.sqrt(HD)

    mid_row, mid_col = iota((ROWS, 2 * ROWS), 0), iota((ROWS, 2 * ROWS), 1)
    from_row = (mid_row & (NZ - 1)) * 16 + lax.shift_right_logical(mid_row, 4)
    mid_left = one_hot(mid_col == from_row)
    mid_right = one_hot(mid_col == from_row + 8)

    def cross_head(h, carry):
        cols = pl.ds(pl.multiple_of(h * HD, HD), HD)
        query = packed[T, :, cols]
        scores = jnp.where(
            earlier_text, dot_t(query, txt[0, 0, 0, :, cols]), dot_t(query, txt[1, 0, 0, :, cols])
        )
        top = jnp.max(scores, axis=1, keepdims=True)
        expo = jnp.exp2((scores - top) * scale)
        total = jnp.sum(expo, axis=1, keepdims=True)
        weights = expo.astype(BF16)
        out = jnp.where(
            earlier, dot(weights, txt[0, 1, 0, :, cols]), dot(weights, txt[1, 1, 0, :, cols])
        )
        cross[:, cols] = out / total
        return carry

    def self_head(h, carry):
        cols = pl.ds(pl.multiple_of(h * HD, HD), HD)
        query = packed[Q, :, cols]
        own_scores = jnp.where(mask_own, dot_t(query, packed[K, :, cols]), -1e30)
        near = jnp.where(earlier, dot_t(query, kv_prev[0, :, cols]), dot_t(query, kv_next[0, :, cols]))
        near = jnp.where(mask_near, near, -1e30)
        top = jnp.max(jnp.maximum(own_scores, near), axis=1, keepdims=True)
        own_expo = jnp.exp2((own_scores - top) * scale)
        near_expo = jnp.exp2((near - top) * scale)
        total = jnp.sum(own_expo + near_expo, axis=1, keepdims=True)
        near_weights = near_expo.astype(BF16)
        out = dot(own_expo.astype(BF16), packed[V, :, cols])
        out = out + jnp.where(
            earlier, dot(near_weights, kv_prev[1, :, cols]), dot(near_weights, kv_next[1, :, cols])
        )
        o_ref[:, cols] = (out / total + cross[:, cols]).astype(BF16)
        return carry

    for c, (a, first, columns) in enumerate(CHUNKS):
        half = columns // 2
        bytes_of(zrecv[c].at[pl.ds(0, NZ - 1)], z_ssem.at[c], z_rsem.at[c]).wait_recv()
        arrived = zrecv[c][...].reshape(2 * ROWS, half)
        xsend[c][:, :, :half] = dot(mid_left, arrived).astype(BF16).reshape(NW, NZ, half)
        xsend[c][:, :, half:] = dot(mid_right, arrived).astype(BF16).reshape(NW, NZ, half)

        def send_x(i, carry):
            to = lax.rem(w + i, NW)
            remote(xsend[c].at[to], xrecv[c].at[w], x_ssem.at[c], x_rsem.at[c], w_device(to)).start()
            return carry

        lax.fori_loop(1, NW, send_x, 0)
        xrecv[c][w] = xsend[c][w]
        bytes_of(xrecv[c].at[pl.ds(0, NW - 1)], x_ssem.at[c], x_rsem.at[c]).wait_recv()
        packed[a, :, first : first + columns] = dot(place, xrecv[c][...].reshape(ROWS, columns)).astype(BF16)
        if a in (K, V):
            i = a - K
            remote(packed.at[a], kv_prev.at[i], n_ssem.at[2 * i], n_rsem.at[2 * i], after).start()
            remote(packed.at[a], kv_next.at[i], n_ssem.at[2 * i + 1], n_rsem.at[2 * i + 1], before).start()
        elif a == T:
            own_text.wait()
            for i in range(2):
                bytes_of(txt.at[0, i], t_ssem.at[i], t_rsem.at[i]).wait_recv()
            lax.fori_loop(0, HEADS, cross_head, 0)
        else:
            if first == 0:
                for i in range(2):
                    bytes_of(kv_prev.at[i], n_ssem.at[2 * i], n_rsem.at[2 * i]).wait_recv()
                    bytes_of(kv_next.at[i], n_ssem.at[2 * i + 1], n_rsem.at[2 * i + 1]).wait_recv()
            lax.fori_loop(first // HD, (first + columns) // HD, self_head, 0)

    bytes_of(slot_send.at[pl.ds(0, NZ - 1)], s_sems.at[0], s_sems.at[1]).wait_send()
    bytes_of(row_recv.at[pl.ds(0, NW - 1)], s_sems.at[2], s_sems.at[3]).wait_send()
    for i in range(2):
        bytes_of(img_near.at[i], i_sems.at[2 * i], i_sems.at[2 * i + 1]).wait_send()
        bytes_of(txt.at[0, i], t_ssem.at[i], t_rsem.at[i]).wait_send()
        bytes_of(kv_prev.at[i], n_ssem.at[2 * i], n_rsem.at[2 * i]).wait_send()
        bytes_of(kv_next.at[i], n_ssem.at[2 * i + 1], n_rsem.at[2 * i + 1]).wait_send()
    for c in range(NC):
        bytes_of(ybuf[c].at[pl.ds(0, 96)], y_ssem.at[c], y_rsem.at[c]).wait_send()
        bytes_of(zsend[c].at[pl.ds(0, NZ - 1)], z_ssem.at[c], z_rsem.at[c]).wait_send()
        bytes_of(xsend[c].at[pl.ds(0, NW - 1)], x_ssem.at[c], x_rsem.at[c]).wait_send()


def body(queries, keys, values, text_queries, text_states, packed_pos, image_of):
    dma = pltpu.SemaphoreType.DMA
    scratch = []
    scratch += [pltpu.VMEM((ROWS, n), BF16) for _, _, n in CHUNKS]
    scratch += [pltpu.VMEM((NZ, 16, n // 2), BF16) for _, _, n in CHUNKS] * 2
    scratch += [pltpu.VMEM((NW, NZ, n), BF16) for _, _, n in CHUNKS] * 2
    scratch += [
        pltpu.VMEM((4, ROWS, FEAT), BF16),
        pltpu.VMEM((2, ROWS, FEAT), BF16),
        pltpu.VMEM((2, ROWS, FEAT), BF16),
        pltpu.VMEM((2, 2, 1, TXT, FEAT), BF16),
        pltpu.VMEM((ROWS, FEAT), F32),
        pltpu.VMEM((NZ, 1, ROWS), I32),
        pltpu.VMEM((NZ, 1, ROWS), I32),
        pltpu.VMEM((1, ROWS), I32),
        pltpu.VMEM((NW, 1, ROWS), I32),
        pltpu.VMEM((2, 1, ROWS), I32),
    ]
    scratch += [dma((NC + 1,))] + [dma((NC,))] * 6 + [dma((4,)), dma((4,)), dma((2,)), dma((2,)), dma((4,)), dma((4,))]
    hbm = pl.BlockSpec(memory_space=pl.ANY)
    vmem = pl.BlockSpec(memory_space=pltpu.VMEM)
    return pl.pallas_call(
        kernel,
        out_shape=jax.ShapeDtypeStruct((ROWS, FEAT), BF16),
        in_specs=[hbm] * 5 + [vmem] * 2,
        out_specs=vmem,
        scratch_shapes=scratch,
        compiler_params=pltpu.CompilerParams(collective_id=0, has_side_effects=True, vmem_limit_bytes=48 * 2**20),
    )(queries, keys, values, text_queries, text_states, packed_pos.reshape(1, ROWS), image_of.reshape(1, ROWS))


def solution(mesh):
    return jax.shard_map(
        body,
        mesh=mesh,
        in_specs=(
            P(("seq", "mp"), None),
            P(("seq", "mp"), None),
            P(("seq", "mp"), None),
            P(("seq", "mp"), None),
            P(None, "seq", None, "mp"),
            P("seq"),
            P("seq"),
        ),
        out_specs=P("seq", "mp"),
        check_vma=False,
    )
```

time: 210 us -> 102 us (0.49)
  the two profiles are of different devices: /device:TPU:103 before, /device:TPU:1 now
where the time goes in v1:
time: 102 us
  Pallas kernels  99.7 us (98%)
  local copies, waits for them, and re-layouts  2.42 us (2%)
    pallas_call x1, Pallas kernels, body(): pl.pallas_call(kernel, out_shape=jax.ShapeDtypeStruct((ROWS, FEAT), BF16)...  99.7 us
    unnamed x14, local copies, waits for them, and re-layouts  2.42 us

profile of v1, /device:TPU:1, one launch (start us, length us, event | category | flops | bytes accessed | tf_op | source)
XLA Modules:
  0.0 102.2 jit_solution(9462129911696474788)
XLA Ops:
  0.0 0.0 copy-start.5
  0.0 0.0 copy-start.4
  0.0 0.0 copy-start.3
  0.0 0.0 copy-start.2
  0.0 0.0 copy-start.1
  0.0 0.0 copy-start
  0.0 1.7 %copy.8.text_ref = bf16[2,1,300,1024]{3,2,1,0:T(8,128)(2,1)S(1)} copy(bf16[2,1,300,1024]{3,0,2,1:T(2,128)(2,1)} %param.11) | data formatting | bytes 2457600 | tf_op args[4]
  1.7 0.0 copy-done.5
  1.7 0.0 copy-done.4
  1.8 0.0 copy-done.3
  1.8 0.0 copy-done.2
  1.8 0.0 copy-done.1
  1.8 0.0 copy-done
  1.8 99.7 %shard_map.73 = bf16[128,1024]{1,0:T(8,128)(2,1)S(1)} custom-call(bf16[32,4096]{1,0:T(8,128)(2,1)S(1)} %copy-done, bf16[32,4096]{1,0:T(8,128)(2,1)S(1)} %copy-done.1, bf16[32,4096]{1,0:T(8,128)(2,1)S(1)} %copy-done.2, bf16[32,4096]{1,0:T(8,128)(2,1)S(1)} %copy-done.3, bf16[2,1,300,1024]{3,2,1,0:T(8,128)(2,1)S(1)} %copy.8.text_ref, s32[1,128]{1,0:T(1,128)S(1)} %bitcast.2, ...), custom_call_target="tpu_custom_call" | custom-call | tf_op jit(solution)/shard_map/pallas_call | solution.py:298
  101.5 0.7 copy.10
Async XLA Ops:
  0.0 1.7 %copy-start.5 = (s32[128]{0:T(128)S(1)}, s32[128]{0:T(128)}, u32[]{:S(2)}) copy-start(s32[128]{0:T(128)} %param.13) | copy-start | bytes 1540
  0.0 1.7 %copy-start.4 = (s32[128]{0:T(128)S(1)}, s32[128]{0:T(128)}, u32[]{:S(2)}) copy-start(s32[128]{0:T(128)} %param.12) | copy-start | bytes 1540
  0.0 1.8 %copy-start.3 = (bf16[32,4096]{1,0:T(8,128)(2,1)S(1)}, bf16[32,4096]{1,0:T(8,128)(2,1)}, u32[]{:S(2)}) copy-start(bf16[32,4096]{1,0:T(8,128)(2,1)} %t_ref.1) | copy-start | bytes 786436
  0.0 1.8 %copy-start.2 = (bf16[32,4096]{1,0:T(8,128)(2,1)S(1)}, bf16[32,4096]{1,0:T(8,128)(2,1)}, u32[]{:S(2)}) copy-start(bf16[32,4096]{1,0:T(8,128)(2,1)} %v_ref.1) | copy-start | bytes 786436
  0.0 1.8 %copy-start.1 = (bf16[32,4096]{1,0:T(8,128)(2,1)S(1)}, bf16[32,4096]{1,0:T(8,128)(2,1)}, u32[]{:S(2)}) copy-start(bf16[32,4096]{1,0:T(8,128)(2,1)} %k_ref.1) | copy-start | bytes 786436
  0.0 1.8 %copy-start = (bf16[32,4096]{1,0:T(8,128)(2,1)S(1)}, bf16[32,4096]{1,0:T(8,128)(2,1)}, u32[]{:S(2)}) copy-start(bf16[32,4096]{1,0:T(8,128)(2,1)} %q_ref.1) | copy-start | bytes 786436

commit v2 on v1

v2 whole, which is shorter than its diff:
```python
import functools
import math

import jax
import jax.numpy as jnp
from jax import lax
from jax.experimental import pallas as pl
from jax.experimental.pallas import tpu as pltpu
from jax.sharding import PartitionSpec as P

MESH = pl.DeviceIdType.MESH
HD = 128
ROWS = 128
NZ = 16
NW = 8
NY = 4
FEAT = 1024
HEADS = 8
TXT = 300
TXT_PAD = 304
TXT_ROWS = TXT * 2 * HEADS
PIECE = TXT_ROWS // 4
Q, K, V, T = 0, 1, 2, 3
CHUNKS = (
    (K, 0, 512),
    (K, 512, 512),
    (V, 0, 512),
    (V, 512, 512),
    (T, 0, 512),
    (T, 512, 512),
    (Q, 0, 512),
    (Q, 512, 512),
)
NC = len(CHUNKS)
Y_AHEAD = 2
Z_FIRST = 2
F32 = jnp.float32
BF16 = jnp.bfloat16
I32 = jnp.int32


def iota(shape, dim):
    return lax.broadcasted_iota(I32, shape, dim)


def one_hot(condition):
    return jnp.where(condition, 1.0, 0.0).astype(BF16)


def dot(a, b):
    return jnp.dot(a, b, preferred_element_type=F32)


def dot_t(a, b):
    return lax.dot_general(a, b, (((1,), (1,)), ((), ())), preferred_element_type=F32)


def kernel(q_ref, k_ref, v_ref, t_ref, text_ref, pos_ref, img_ref, o_ref, *scratch):
    scratch = list(scratch)
    take = lambda n: [scratch.pop(0) for _ in range(n)]
    ybuf, zsend, zrecv, xsend, xrecv = (take(NC) for _ in range(5))
    (packed, kv, relay, raw, txt, cross, slot_send, slot_recv, row_send, row_recv, img_near) = take(11)
    (local_sem, y_ssem, y_rsem, z_ssem, z_rsem, x_ssem, x_rsem, n_ssem, n_rsem, t_ssem, t_rsem, s_sems, i_sems) = take(13)
    arrays = (q_ref, k_ref, v_ref, t_ref)

    me = lax.axis_index("seq")
    y = lax.axis_index("mp")
    z, w = me // NW, me % NW
    z_device = lambda other: {"seq": other * NW + w}
    w_device = lambda other: {"seq": z * NW + other}
    after = {"seq": lax.rem(me + 1, NZ * NW)}
    before = {"seq": lax.rem(me + NZ * NW - 1, NZ * NW)}

    def remote(src, dst, send, recv, device):
        return pltpu.make_async_remote_copy(
            src_ref=src, dst_ref=dst, send_sem=send, recv_sem=recv, device_id=device, device_id_type=MESH
        )

    def bytes_of(ref, send, recv):
        return remote(ref, ref, send, recv, after)

    barrier = pltpu.get_barrier_semaphore()
    for i in range(1, NY):
        pl.semaphore_signal(barrier, inc=1, device_id={"mp": lax.rem(y + i, NY)}, device_id_type=MESH)

    def greet_z(i, carry):
        pl.semaphore_signal(barrier, inc=1, device_id=z_device(lax.rem(z + i, NZ)), device_id_type=MESH)
        return carry

    lax.fori_loop(1, NZ, greet_z, 0)

    def greet_w(i, carry):
        pl.semaphore_signal(barrier, inc=1, device_id=w_device(lax.rem(w + i, NW)), device_id_type=MESH)
        return carry

    lax.fori_loop(1, NW, greet_w, 0)
    for device in (after, before):
        pl.semaphore_signal(barrier, inc=1, device_id=device, device_id_type=MESH)

    own = []
    for c, (a, first, columns) in enumerate(CHUNKS):
        start = pl.multiple_of(y * FEAT + first, 128)
        own.append(
            pltpu.make_async_copy(
                arrays[a].at[:, pl.ds(start, columns)], ybuf[c].at[pl.ds(pl.multiple_of(y * 32, 32), 32)], local_sem.at[c]
            )
        )
        own[-1].start()
    own_text = pltpu.make_async_copy(text_ref, raw.at[1], local_sem.at[NC])
    own_text.start()

    pos = pos_ref[...]
    target = lax.shift_right_logical(pos, 7)
    slot = pos & (ROWS - 1)
    image = img_ref[...]
    out_row = iota((2 * ROWS, ROWS), 0)
    same = (lax.shift_right_logical(out_row, 4) * NW + (out_row & 7)) == target
    right_half = (out_row & 8) == 8
    send_plane = one_hot(iota((ROWS, ROWS), 0) == (target & 7) * NZ + lax.shift_right_logical(target, 3))
    send_left = one_hot(same & ~right_half)
    send_right = one_hot(same & right_half)
    to_z = one_hot(iota((NZ, ROWS), 0) == lax.shift_right_logical(target, 3))
    lane_of = (target & 7) * NZ + z
    by_lane = jnp.where(iota((ROWS, ROWS), 0) == lane_of, slot.astype(F32), 0.0).astype(BF16)
    slots = dot_t(to_z, by_lane).astype(I32)
    for i in range(NZ):
        slot_send[i] = slots[i : i + 1]

    with jax.named_scope("greeting"):
        pl.semaphore_wait(barrier, NY - 1 + NZ - 1 + NW - 1 + 2)

    def send_y(c):
        a, first, columns = CHUNKS[c]
        for i in range(1, NY):
            other = lax.rem(y + i, NY)
            start = pl.multiple_of(other * FEAT + first, 128)
            remote(
                arrays[a].at[:, pl.ds(start, columns)],
                ybuf[c].at[pl.ds(pl.multiple_of(y * 32, 32), 32)],
                y_ssem.at[c],
                y_rsem.at[c],
                {"mp": other},
            ).start()

    for c in range(Y_AHEAD):
        send_y(c)

    @pl.when(w < NW - 1)
    def _():
        remote(text_ref, raw.at[0], t_ssem.at[0], t_rsem.at[0], after).start()

    @pl.when(w == NW - 1)
    def _():
        for j in range(3):
            remote(
                text_ref.at[pl.ds(j * PIECE, PIECE)], relay.at[0], t_ssem.at[1], t_rsem.at[1], w_device(2 * j + 1)
            ).start()
        remote(
            text_ref.at[pl.ds(3 * PIECE, PIECE)], relay.at[1], t_ssem.at[2], t_rsem.at[2], z_device(lax.rem(z + 1, NZ))
        ).start()

    def relay_up():
        @pl.when((w % 2 == 1) & (w < NW - 1))
        def _():
            bytes_of(relay.at[0], t_ssem.at[1], t_rsem.at[1]).wait_recv()
            remote(relay.at[0], relay.at[1], t_ssem.at[2], t_rsem.at[2], z_device(lax.rem(z + 1, NZ))).start()

    def relay_in():
        @pl.when(w % 2 == 1)
        def _():
            bytes_of(relay.at[1], t_ssem.at[2], t_rsem.at[2]).wait_recv()
            piece = raw.at[0, pl.ds(pl.multiple_of((w // 2) * PIECE, 16), PIECE)]
            remote(relay.at[1], piece, t_ssem.at[3], t_rsem.at[0], w_device(0)).start()

    def far_first(i):
        return lax.rem(z + 8 + jnp.where(i % 2 == 0, -(i // 2), i // 2), NZ)

    def send_slots(i, carry):
        to = far_first(i)
        remote(slot_send.at[to], slot_recv.at[z], s_sems.at[0], s_sems.at[1], z_device(to)).start()
        return carry

    lax.fori_loop(1, NZ, send_slots, 0)
    slot_recv[z] = slot_send[z]
    remote(img_ref, img_near.at[0], i_sems.at[0], i_sems.at[1], after).start()
    remote(img_ref, img_near.at[1], i_sems.at[2], i_sems.at[3], before).start()

    def after_y(c):
        with jax.named_scope(f"mp_arrival_{c}"):
            own[c].wait()
            bytes_of(ybuf[c].at[pl.ds(0, 96)], y_ssem.at[c], y_rsem.at[c]).wait_recv()
        if c + Y_AHEAD < NC:
            send_y(c + Y_AHEAD)

    def over_z(c, left, right, rows):
        half = CHUNKS[c][2] // 2
        out = dot(left, rows[:, :half]) + dot(right, rows[:, half:])
        zsend[c][...] = out.astype(BF16).reshape(NZ, 16, half)

        def send_z(i, carry):
            to = far_first(i)
            remote(zsend[c].at[to], zrecv[c].at[z], z_ssem.at[c], z_rsem.at[c], z_device(to)).start()
            return carry

        lax.fori_loop(1, NZ, send_z, 0)
        zrecv[c][z] = zsend[c][z]

    def over_plane(c):
        def send_x(i, carry):
            to = lax.rem(w + i, NW)
            remote(xsend[c].at[to], xrecv[c].at[w], x_ssem.at[c], x_rsem.at[c], w_device(to)).start()
            return carry

        lax.fori_loop(1, NW, send_x, 0)
        xrecv[c][w] = xsend[c][w]

    def plane_first(c):
        after_y(c)
        xsend[c][...] = dot(send_plane, ybuf[c][...]).astype(BF16).reshape(NW, NZ, CHUNKS[c][2])
        over_plane(c)

    def from_plane(c):
        with jax.named_scope(f"plane_arrival_{c}"):
            bytes_of(xrecv[c].at[pl.ds(0, NW - 1)], x_ssem.at[c], x_rsem.at[c]).wait_recv()
        return xrecv[c][...].reshape(ROWS, CHUNKS[c][2])

    for c in range(Z_FIRST):
        after_y(c)
        over_z(c, send_left, send_right, ybuf[c][...])
    plane_first(Z_FIRST)
    relay_up()

    by_head_row, by_head_col = iota((256, 256), 0), iota((256, 256), 1)
    by_head = one_hot(
        by_head_col
        == (by_head_row & 15) * 16 + lax.shift_right_logical(by_head_row, 5) * 2 + (lax.shift_right_logical(by_head_row, 4) & 1)
    )

    def sort_prompt(p):
        def two_groups(g, carry):
            first = raw[p, pl.ds(pl.multiple_of(g * 512, 512), 256)]
            second = raw[p, pl.ds(pl.multiple_of(g * 512 + 256, 256), 256)]
            out = dot(by_head, jnp.concatenate([first, second], axis=1)).astype(BF16)
            for i in range(2):
                place_at = pl.ds(pl.multiple_of(g * 32 + 16 * i, 16), 16)
                txt[p, :, :, place_at, :] = out[:, i * HD : (i + 1) * HD].reshape(HEADS, 2, 16, HD)
            return carry

        lax.fori_loop(0, 9, two_groups, 0)
        out = dot(by_head[:, :192], raw[p, 4608:4800]).astype(BF16)
        txt[p, :, :, 288:304, :] = out.reshape(HEADS, 2, 16, HD)

    with jax.named_scope("own_prompt"):
        own_text.wait()
        sort_prompt(1)

    bytes_of(slot_recv.at[pl.ds(0, NZ - 1)], s_sems.at[0], s_sems.at[1]).wait_recv()
    row = slot_recv[0]
    for i in range(1, NZ):
        row = row + slot_recv[i]
    row_send[...] = row

    def send_row(i, carry):
        to = lax.rem(w + i, NW)
        remote(row_send, row_recv.at[w], s_sems.at[2], s_sems.at[3], w_device(to)).start()
        return carry

    lax.fori_loop(1, NW, send_row, 0)
    row_recv[w] = row
    bytes_of(row_recv.at[pl.ds(0, NW - 1)], s_sems.at[2], s_sems.at[3]).wait_recv()
    rows = jnp.concatenate([row_recv[i] for i in range(NW)], axis=0)
    pick = one_hot(iota((ROWS, ROWS), 0) == w * NZ + (iota((ROWS, ROWS), 1) & (NZ - 1)))
    landed = dot(rows.astype(F32).astype(BF16), pick)
    mine = lax.shift_right_logical(iota((NW, ROWS), 1), 4) == iota((NW, ROWS), 0)
    landing = jnp.sum(jnp.where(mine, landed, 0.0), axis=0, keepdims=True).astype(I32)
    place = one_hot(iota((ROWS, ROWS), 0) == landing)

    count = lambda flags: jnp.sum(jnp.where(flags, 1.0, 0.0), axis=1, keepdims=True).astype(I32)
    for i in range(2):
        bytes_of(img_near.at[i], i_sems.at[2 * i], i_sems.at[2 * i + 1]).wait_recv()
    cut = count(image < me)
    cut_prev = count(img_near[0] < me - 1)
    cut_next = count(img_near[1] == me)
    earlier = iota((ROWS, ROWS), 0) < cut
    query_row, key_row = iota((ROWS, 3 * ROWS), 0), iota((ROWS, 3 * ROWS), 1)
    mask = ((query_row < cut) & (key_row >= cut_prev) & (key_row < ROWS + cut)) | (
        (query_row >= cut) & (key_row >= ROWS + cut) & (key_row < 2 * ROWS + cut_next)
    )
    earlier_text = iota((ROWS, TXT_PAD), 0) < cut
    is_text = iota((ROWS, TXT_PAD), 1) < TXT
    scale = math.log2(math.e) / math.sqrt(HD)

    mid_row, mid_col = iota((ROWS, 2 * ROWS), 0), iota((ROWS, 2 * ROWS), 1)
    from_row = (mid_row & (NZ - 1)) * 16 + lax.shift_right_logical(mid_row, 4)
    mid_left = one_hot(mid_col == from_row)
    mid_right = one_hot(mid_col == from_row + 8)
    place_left = dot(place, mid_left).astype(BF16)
    place_right = dot(place, mid_right).astype(BF16)
    row_of, col_of = iota((2 * ROWS, ROWS), 0), iota((2 * ROWS, ROWS), 1)
    to_row = (col_of & (NZ - 1)) * 16 + lax.shift_right_logical(col_of, 4)
    back_left = one_hot(row_of == to_row)
    back_right = one_hot(row_of == to_row + 8)

    def cross_head(h):
        cols = slice(h * HD, (h + 1) * HD)
        query = packed[1, :, cols]
        scores = jnp.where(earlier_text, dot_t(query, txt[0, h, 0]), dot_t(query, txt[1, h, 0]))
        scores = jnp.where(is_text, scores, -1e30)
        top = jnp.max(scores, axis=1, keepdims=True)
        expo = jnp.exp2((scores - top) * scale)
        weights = (expo * (1.0 / jnp.sum(expo, axis=1, keepdims=True))).astype(BF16)
        cross[:, cols] = jnp.where(earlier, dot(weights, txt[0, h, 1]), dot(weights, txt[1, h, 1]))

    ones = jnp.ones((3 * ROWS, HD), BF16)

    def self_head(h):
        cols = slice(h * HD, (h + 1) * HD)
        scores = jnp.where(mask, dot_t(packed[0, :, cols], kv[0, :, cols]), -1e30)
        top = jnp.max(scores, axis=1, keepdims=True)
        weights = jnp.exp2((scores - top) * scale).astype(BF16)
        o_ref[:, cols] = (dot(weights, kv[1, :, cols]) / dot(weights, ones) + cross[:, cols]).astype(BF16)

    near = [c for c, (a, _, _) in enumerate(CHUNKS) if a in (K, V)]

    def near_part(c, side):
        a, first, columns = CHUNKS[c]
        return kv.at[a - K, pl.ds(2 * ROWS * side, ROWS), pl.ds(first, columns)]

    def from_z(c):
        with jax.named_scope(f"z_arrival_{c}"):
            bytes_of(zrecv[c].at[pl.ds(0, NZ - 1)], z_ssem.at[c], z_rsem.at[c]).wait_recv()
        return zrecv[c][...].reshape(2 * ROWS, CHUNKS[c][2] // 2)

    def plane_last(c):
        half = CHUNKS[c][2] // 2
        arrived = from_z(c)
        xsend[c][:, :, :half] = dot(mid_left, arrived).astype(BF16).reshape(NW, NZ, half)
        xsend[c][:, :, half:] = dot(mid_right, arrived).astype(BF16).reshape(NW, NZ, half)
        over_plane(c)

    def use(c, left, right):
        a, first, columns = CHUNKS[c]
        heads = range(first // HD, (first + columns) // HD)
        if a in (K, V):
            kv[a - K, ROWS : 2 * ROWS, first : first + columns // 2] = left
            kv[a - K, ROWS : 2 * ROWS, first + columns // 2 : first + columns] = right
            cols, i = pl.ds(first, columns), near.index(c)
            mine = kv.at[a - K, pl.ds(ROWS, ROWS), cols]
            remote(mine, kv.at[a - K, pl.ds(0, ROWS), cols], n_ssem.at[2 * i], n_rsem.at[2 * i], after).start()
            remote(mine, kv.at[a - K, pl.ds(2 * ROWS, ROWS), cols], n_ssem.at[2 * i + 1], n_rsem.at[2 * i + 1], before).start()
            return
        packed[int(a == T), :, first : first + columns // 2] = left
        packed[int(a == T), :, first + columns // 2 : first + columns] = right
        if a == T:
            if first == 0:
                with jax.named_scope("prompt_arrival"):
                    bytes_of(raw.at[0], t_ssem.at[0], t_rsem.at[0]).wait_recv()
                with jax.named_scope("earlier_prompt"):
                    sort_prompt(0)
            with jax.named_scope("cross_attention"):
                for h in heads:
                    cross_head(h)
            return
        if first == 0:
            with jax.named_scope("near_arrival"):
                for i, n in enumerate(near):
                    for side in range(2):
                        bytes_of(near_part(n, side), n_ssem.at[2 * i + side], n_rsem.at[2 * i + side]).wait_recv()
        with jax.named_scope(f"self_attention_{c}"):
            for h in heads:
                self_head(h)

    def use_from_plane(c):
        rows = from_plane(c)
        half = CHUNKS[c][2] // 2
        use(c, dot(place, rows[:, :half]).astype(BF16), dot(place, rows[:, half:]).astype(BF16))

    for c in range(NC):
        if c < Z_FIRST:
            plane_last(c)
        else:
            arrived = from_z(c)
        if c + Z_FIRST < NC:
            over_z(c + Z_FIRST, back_left, back_right, from_plane(c + Z_FIRST))
        if c + Z_FIRST + 1 < NC:
            plane_first(c + Z_FIRST + 1)
        if c == 1:
            relay_in()
        if 0 < c <= Z_FIRST:
            use_from_plane(c - 1)
        if c >= Z_FIRST:
            use(c, dot(place_left, arrived).astype(BF16), dot(place_right, arrived).astype(BF16))

    @pl.when(w < NW - 1)
    def _():
        bytes_of(raw.at[0], t_ssem.at[0], t_rsem.at[0]).wait_send()

    @pl.when(w == NW - 1)
    def _():
        bytes_of(raw.at[0, pl.ds(0, 3 * PIECE)], t_ssem.at[1], t_rsem.at[1]).wait_send()

    @pl.when(w % 2 == 1)
    def _():
        bytes_of(relay.at[1], t_ssem.at[2], t_rsem.at[2]).wait_send()
        bytes_of(relay.at[1], t_ssem.at[3], t_rsem.at[3]).wait_send()

    bytes_of(slot_send.at[pl.ds(0, NZ - 1)], s_sems.at[0], s_sems.at[1]).wait_send()
    bytes_of(row_recv.at[pl.ds(0, NW - 1)], s_sems.at[2], s_sems.at[3]).wait_send()
    for i in range(2):
        bytes_of(img_near.at[i], i_sems.at[2 * i], i_sems.at[2 * i + 1]).wait_send()
    for i, n in enumerate(near):
        for side in range(2):
            bytes_of(near_part(n, side), n_ssem.at[2 * i + side], n_rsem.at[2 * i + side]).wait_send()
    for c in range(NC):
        bytes_of(ybuf[c].at[pl.ds(0, 96)], y_ssem.at[c], y_rsem.at[c]).wait_send()
        bytes_of(zsend[c].at[pl.ds(0, NZ - 1)], z_ssem.at[c], z_rsem.at[c]).wait_send()
        bytes_of(xsend[c].at[pl.ds(0, NW - 1)], x_ssem.at[c], x_rsem.at[c]).wait_send()


def body(queries, keys, values, text_queries, text_states, packed_pos, image_of):
    dma = pltpu.SemaphoreType.DMA
    scratch = []
    scratch += [pltpu.VMEM((ROWS, n), BF16) for _, _, n in CHUNKS]
    scratch += [pltpu.VMEM((NZ, 16, n // 2), BF16) for _, _, n in CHUNKS] * 2
    scratch += [pltpu.VMEM((NW, NZ, n), BF16) for _, _, n in CHUNKS] * 2
    scratch += [
        pltpu.VMEM((2, ROWS, FEAT), BF16),
        pltpu.VMEM((2, 3 * ROWS, FEAT), BF16),
        pltpu.VMEM((2, PIECE, HD), BF16),
        pltpu.VMEM((2, TXT_ROWS, HD), BF16),
        pltpu.VMEM((2, HEADS, 2, TXT_PAD, HD), BF16),
        pltpu.VMEM((ROWS, FEAT), F32),
        pltpu.VMEM((NZ, 1, ROWS), I32),
        pltpu.VMEM((NZ, 1, ROWS), I32),
        pltpu.VMEM((1, ROWS), I32),
        pltpu.VMEM((NW, 1, ROWS), I32),
        pltpu.VMEM((2, 1, ROWS), I32),
    ]
    scratch += [dma((NC + 1,))] + [dma((NC,))] * 6 + [dma((2 * NC,))] * 2 + [dma((4,))] * 4
    hbm = pl.BlockSpec(memory_space=pl.ANY)
    vmem = pl.BlockSpec(memory_space=pltpu.VMEM)
    prompt = text_states.transpose(1, 2, 0, 3).reshape(TXT, 2, HEADS, HD).transpose(0, 2, 1, 3).reshape(TXT_ROWS, HD)
    return pl.pallas_call(
        kernel,
        out_shape=jax.ShapeDtypeStruct((ROWS, FEAT), BF16),
        in_specs=[hbm] * 5 + [vmem] * 2,
        out_specs=vmem,
        scratch_shapes=scratch,
        compiler_params=pltpu.CompilerParams(collective_id=0, has_side_effects=True, vmem_limit_bytes=60 * 2**20),
    )(queries, keys, values, text_queries, prompt, packed_pos.reshape(1, ROWS), image_of.reshape(1, ROWS))


def solution(mesh):
    return jax.shard_map(
        body,
        mesh=mesh,
        in_specs=(
            P(("seq", "mp"), None),
            P(("seq", "mp"), None),
            P(("seq", "mp"), None),
            P(("seq", "mp"), None),
            P(None, "seq", None, "mp"),
            P("seq"),
            P("seq"),
        ),
        out_specs=P("seq", "mp"),
        check_vma=False,
    )
```

time: 102 us -> 82.2 us (0.81)
  the two profiles are of different devices: /device:TPU:1 before, /device:TPU:8 now
where the time goes in v2:
time: 82.2 us; the launch traced here: 82.1 us
  Pallas kernels  80.4 us (98%)
  local copies, waits for them, and re-layouts  1.67 us (2%)
    pallas_call x1, Pallas kernels, body(): pl.pallas_call(kernel, out_shape=jax.ShapeDtypeStruct((ROWS, FEAT), BF16)...  80.4 us
    unnamed x1, local copies, waits for them, and re-layouts  1.67 us

profile of v2, /device:TPU:8, one launch (start us, length us, event | category | flops | bytes accessed | tf_op | source)
XLA Modules:
  0.0 82.1 jit_solution(13064247765626373920)
XLA Ops:
  0.0 80.4 %shard_map.73 = bf16[128,1024]{1,0:T(8,128)(2,1)} custom-call(bf16[32,4096]{1,0:T(8,128)(2,1)} %q_ref.1, bf16[32,4096]{1,0:T(8,128)(2,1)} %k_ref.1, bf16[32,4096]{1,0:T(8,128)(2,1)} %v_ref.1, bf16[32,4096]{1,0:T(8,128)(2,1)} %t_ref.1, bf16[4800,128]{1,0:T(8,128)(2,1)} %bitcast.9, s32[1,128]{1,0:T(1,128)} %bitcast.10, s32[1,128]{1,0:T(1,128)} %bitcast.11), custom_call_target="tpu_custom_call" | custom-call | tf_op jit(solution)/shard_map/pallas_call | solution.py:443
  80.4 1.7 %copy.10 = bf16[128,1024]{1,0:T(8,128)(2,1)} copy(bf16[128,1024]{1,0:T(8,128)(2,1)} %shard_map.73) | data formatting | bytes 524288

commit v3 on v2

--- a/solution.py
+++ b/solution.py
@@ -33,7 +33,7 @@
 )
 NC = len(CHUNKS)
 Y_AHEAD = 2
-Z_FIRST = 2
+Z_FIRST = 3
 F32 = jnp.float32
 BF16 = jnp.bfloat16
 I32 = jnp.int32
@@ -59,8 +59,8 @@
     scratch = list(scratch)
     take = lambda n: [scratch.pop(0) for _ in range(n)]
     ybuf, zsend, zrecv, xsend, xrecv = (take(NC) for _ in range(5))
-    (packed, kv, relay, raw, txt, cross, slot_send, slot_recv, row_send, row_recv, img_near) = take(11)
-    (local_sem, y_ssem, y_rsem, z_ssem, z_rsem, x_ssem, x_rsem, n_ssem, n_rsem, t_ssem, t_rsem, s_sems, i_sems) = take(13)
+    (packed, kv, relay, near_relay, raw, txt, cross, slot_send, slot_recv, row_send, row_recv, img_near) = take(12)
+    (local_sem, y_ssem, y_rsem, z_ssem, z_rsem, x_ssem, x_rsem, n_ssem, n_rsem, t_ssem, t_rsem, s_sems, i_sems, r_sems) = take(14)
     arrays = (q_ref, k_ref, v_ref, t_ref)
 
     me = lax.axis_index("seq")
@@ -96,6 +96,23 @@
     lax.fori_loop(1, NW, greet_w, 0)
     for device in (after, before):
         pl.semaphore_signal(barrier, inc=1, device_id=device, device_id_type=MESH)
+
+    up = {"seq": lax.rem(z + 1, NZ) * NW}
+    down = {"seq": lax.rem(z + NZ - 1, NZ) * NW + NW - 1}
+
+    @pl.when(w == 0)
+    def _():
+        for i in (1, 3, 5):
+            pl.semaphore_signal(
+                barrier, inc=1, device_id={"seq": lax.rem(z + NZ - 1, NZ) * NW + i}, device_id_type=MESH
+            )
+
+    @pl.when(w == NW - 1)
+    def _():
+        for i in (2, 4, 6):
+            pl.semaphore_signal(barrier, inc=1, device_id={"seq": lax.rem(z + 1, NZ) * NW + i}, device_id_type=MESH)
+
+    inner = (w > 0) & (w < NW - 1)
 
     own = []
     for c, (a, first, columns) in enumerate(CHUNKS):
@@ -108,6 +125,61 @@
         own[-1].start()
     own_text = pltpu.make_async_copy(text_ref, raw.at[1], local_sem.at[NC])
     own_text.start()
+
+    with jax.named_scope("greeting"):
+        pl.semaphore_wait(barrier, NY - 1 + NZ - 1 + NW - 1 + 2 + jnp.minimum(w, 1) * jnp.minimum(NW - 1 - w, 1))
+
+    def send_y(c):
+        a, first, columns = CHUNKS[c]
+        for i in range(1, NY):
+            other = lax.rem(y + i, NY)
+            start = pl.multiple_of(other * FEAT + first, 128)
+            remote(
+                arrays[a].at[:, pl.ds(start, columns)],
+                ybuf[c].at[pl.ds(pl.multiple_of(y * 32, 32), 32)],
+                y_ssem.at[c],
+                y_rsem.at[c],
+                {"mp": other},
+            ).start()
+
+    for c in range(Y_AHEAD):
+        send_y(c)
+
+    @pl.when(w < NW - 1)
+    def _():
+        remote(text_ref, raw.at[0], t_ssem.at[0], t_rsem.at[0], after).start()
+
+    @pl.when(w == NW - 1)
+    def _():
+        for j in range(3):
+            remote(text_ref.at[pl.ds(j * PIECE, PIECE)], relay, t_ssem.at[1], t_rsem.at[1], w_device(2 * j + 1)).start()
+        remote(
+            text_ref.at[pl.ds(3 * PIECE, PIECE)], raw.at[0, pl.ds(3 * PIECE, PIECE)], t_ssem.at[2], t_rsem.at[0], after
+        ).start()
+
+    def relay_prompt():
+        @pl.when((w % 2 == 1) & inner)
+        def _():
+            bytes_of(relay, t_ssem.at[1], t_rsem.at[1]).wait_recv()
+            piece = raw.at[0, pl.ds(pl.multiple_of((w // 2) * PIECE, 16), PIECE)]
+            remote(relay, piece, t_ssem.at[2], t_rsem.at[0], up).start()
+
+    def relay_near():
+        def forward(device, side):
+            i = w // 2
+            cols = pl.ds(pl.multiple_of((i % 2) * 512, 512), 512)
+            bytes_of(near_relay, r_sems.at[0], r_sems.at[1]).wait_recv()
+            remote(
+                near_relay, kv.at[i // 2, pl.ds(2 * ROWS * side, ROWS), cols], r_sems.at[0], n_rsem.at[2 * i + side], device
+            ).start()
+
+        @pl.when((w % 2 == 1) & inner)
+        def _():
+            forward(up, 0)
+
+        @pl.when((w % 2 == 0) & inner)
+        def _():
+            forward(down, 1)
 
     pos = pos_ref[...]
     target = lax.shift_right_logical(pos, 7)
@@ -126,52 +198,6 @@
     for i in range(NZ):
         slot_send[i] = slots[i : i + 1]
 
-    with jax.named_scope("greeting"):
-        pl.semaphore_wait(barrier, NY - 1 + NZ - 1 + NW - 1 + 2)
-
-    def send_y(c):
-        a, first, columns = CHUNKS[c]
-        for i in range(1, NY):
-            other = lax.rem(y + i, NY)
-            start = pl.multiple_of(other * FEAT + first, 128)
-            remote(
-                arrays[a].at[:, pl.ds(start, columns)],
-                ybuf[c].at[pl.ds(pl.multiple_of(y * 32, 32), 32)],
-                y_ssem.at[c],
-                y_rsem.at[c],
-                {"mp": other},
-            ).start()
-
-    for c in range(Y_AHEAD):
-        send_y(c)
-
-    @pl.when(w < NW - 1)
-    def _():
-        remote(text_ref, raw.at[0], t_ssem.at[0], t_rsem.at[0], after).start()
-
-    @pl.when(w == NW - 1)
-    def _():
-        for j in range(3):
-            remote(
-                text_ref.at[pl.ds(j * PIECE, PIECE)], relay.at[0], t_ssem.at[1], t_rsem.at[1], w_device(2 * j + 1)
-            ).start()
-        remote(
-            text_ref.at[pl.ds(3 * PIECE, PIECE)], relay.at[1], t_ssem.at[2], t_rsem.at[2], z_device(lax.rem(z + 1, NZ))
-        ).start()
-
-    def relay_up():
-        @pl.when((w % 2 == 1) & (w < NW - 1))
-        def _():
-            bytes_of(relay.at[0], t_ssem.at[1], t_rsem.at[1]).wait_recv()
-            remote(relay.at[0], relay.at[1], t_ssem.at[2], t_rsem.at[2], z_device(lax.rem(z + 1, NZ))).start()
-
-    def relay_in():
-        @pl.when(w % 2 == 1)
-        def _():
-            bytes_of(relay.at[1], t_ssem.at[2], t_rsem.at[2]).wait_recv()
-            piece = raw.at[0, pl.ds(pl.multiple_of((w // 2) * PIECE, 16), PIECE)]
-            remote(relay.at[1], piece, t_ssem.at[3], t_rsem.at[0], w_device(0)).start()
-
     def far_first(i):
         return lax.rem(z + 8 + jnp.where(i % 2 == 0, -(i // 2), i // 2), NZ)
 
@@ -228,7 +254,6 @@
         after_y(c)
         over_z(c, send_left, send_right, ybuf[c][...])
     plane_first(Z_FIRST)
-    relay_up()
 
     by_head_row, by_head_col = iota((256, 256), 0), iota((256, 256), 1)
     by_head = one_hot(
@@ -346,8 +371,29 @@
             kv[a - K, ROWS : 2 * ROWS, first + columns // 2 : first + columns] = right
             cols, i = pl.ds(first, columns), near.index(c)
             mine = kv.at[a - K, pl.ds(ROWS, ROWS), cols]
-            remote(mine, kv.at[a - K, pl.ds(0, ROWS), cols], n_ssem.at[2 * i], n_rsem.at[2 * i], after).start()
-            remote(mine, kv.at[a - K, pl.ds(2 * ROWS, ROWS), cols], n_ssem.at[2 * i + 1], n_rsem.at[2 * i + 1], before).start()
+            to_after = (mine, kv.at[a - K, pl.ds(0, ROWS), cols], n_ssem.at[2 * i], n_rsem.at[2 * i], after)
+            to_before = (mine, kv.at[a - K, pl.ds(2 * ROWS, ROWS), cols], n_ssem.at[2 * i + 1], n_rsem.at[2 * i + 1], before)
+
+            @pl.when((w < NW - 1) | (i == 3))
+            def _():
+                remote(*to_after).start()
+
+            @pl.when((w > 0) | (i == 0))
+            def _():
+                remote(*to_before).start()
+
+            if i < 3:
+
+                @pl.when(w == NW - 1)
+                def _():
+                    remote(mine, near_relay, n_ssem.at[2 * i], r_sems.at[1], w_device(2 * i + 1)).start()
+
+            if i > 0:
+
+                @pl.when(w == 0)
+                def _():
+                    remote(mine, near_relay, n_ssem.at[2 * i + 1], r_sems.at[1], w_device(2 * i)).start()
+
             return
         packed[int(a == T), :, first : first + columns // 2] = left
         packed[int(a == T), :, first + columns // 2 : first + columns] = right
@@ -385,7 +431,9 @@
         if c + Z_FIRST + 1 < NC:
             plane_first(c + Z_FIRST + 1)
         if c == 1:
-            relay_in()
+            relay_prompt()
+        if c == 3:
+            relay_near()
         if 0 < c <= Z_FIRST:
             use_from_plane(c - 1)
         if c >= Z_FIRST:
@@ -401,8 +449,11 @@
 
     @pl.when(w % 2 == 1)
     def _():
-        bytes_of(relay.at[1], t_ssem.at[2], t_rsem.at[2]).wait_send()
-        bytes_of(relay.at[1], t_ssem.at[3], t_rsem.at[3]).wait_send()
+        bytes_of(relay, t_ssem.at[2], t_rsem.at[2]).wait_send()
+
+    @pl.when(inner)
+    def _():
+        bytes_of(near_relay, r_sems.at[0], r_sems.at[1]).wait_send()
 
     bytes_of(slot_send.at[pl.ds(0, NZ - 1)], s_sems.at[0], s_sems.at[1]).wait_send()
     bytes_of(row_recv.at[pl.ds(0, NW - 1)], s_sems.at[2], s_sems.at[3]).wait_send()
@@ -426,7 +477,8 @@
     scratch += [
         pltpu.VMEM((2, ROWS, FEAT), BF16),
         pltpu.VMEM((2, 3 * ROWS, FEAT), BF16),
-        pltpu.VMEM((2, PIECE, HD), BF16),
+        pltpu.VMEM((PIECE, HD), BF16),
+        pltpu.VMEM((ROWS, CHUNKS[0][2]), BF16),
         pltpu.VMEM((2, TXT_ROWS, HD), BF16),
         pltpu.VMEM((2, HEADS, 2, TXT_PAD, HD), BF16),
         pltpu.VMEM((ROWS, FEAT), F32),
@@ -436,7 +488,7 @@
         pltpu.VMEM((NW, 1, ROWS), I32),
         pltpu.VMEM((2, 1, ROWS), I32),
     ]
-    scratch += [dma((NC + 1,))] + [dma((NC,))] * 6 + [dma((2 * NC,))] * 2 + [dma((4,))] * 4
+    scratch += [dma((NC + 1,))] + [dma((NC,))] * 6 + [dma((2 * NC,))] * 2 + [dma((4,))] * 4 + [dma((2,))]
     hbm = pl.BlockSpec(memory_space=pl.ANY)
     vmem = pl.BlockSpec(memory_space=pltpu.VMEM)
     prompt = text_states.transpose(1, 2, 0, 3).reshape(TXT, 2, HEADS, HD).transpose(0, 2, 1, 3).reshape(TXT_ROWS, HD)

time: 82.2 us -> 77.7 us (0.945)
  the two profiles are of different devices: /device:TPU:8 before, /device:TPU:1 now
where the time goes in v3:
time: 77.7 us; the launch traced here: 77.5 us
  Pallas kernels  75.8 us (98%)
  local copies, waits for them, and re-layouts  1.67 us (2%)
    pallas_call x1, Pallas kernels, body(): pl.pallas_call(kernel, out_shape=jax.ShapeDtypeStruct((ROWS, FEAT), BF16)...  75.8 us
    unnamed x1, local copies, waits for them, and re-layouts  1.67 us

profile of v3, /device:TPU:1, one launch (start us, length us, event | category | flops | bytes accessed | tf_op | source)
XLA Modules:
  0.0 77.5 jit_solution(17002446608932570476)
XLA Ops:
  0.0 75.8 %shard_map.73 = bf16[128,1024]{1,0:T(8,128)(2,1)} custom-call(bf16[32,4096]{1,0:T(8,128)(2,1)} %q_ref.1, bf16[32,4096]{1,0:T(8,128)(2,1)} %k_ref.1, bf16[32,4096]{1,0:T(8,128)(2,1)} %v_ref.1, bf16[32,4096]{1,0:T(8,128)(2,1)} %t_ref.1, bf16[4800,128]{1,0:T(8,128)(2,1)} %bitcast.9, s32[1,128]{1,0:T(1,128)} %bitcast.10, s32[1,128]{1,0:T(1,128)} %bitcast.11), custom_call_target="tpu_custom_call" | custom-call | tf_op jit(solution)/shard_map/pallas_call | solution.py:495
  75.9 1.7 %copy.10 = bf16[128,1024]{1,0:T(8,128)(2,1)} copy(bf16[128,1024]{1,0:T(8,128)(2,1)} %shard_map.73) | data formatting | bytes 524288

commit v4 on v3

--- a/solution.py
+++ b/solution.py
@@ -19,7 +19,8 @@
 TXT = 300
 TXT_PAD = 304
 TXT_ROWS = TXT * 2 * HEADS
-PIECE = TXT_ROWS // 4
+PIECE = 592
+OWN_PIECE = TXT_ROWS - 6 * PIECE
 Q, K, V, T = 0, 1, 2, 3
 CHUNKS = (
     (K, 0, 512),
@@ -102,7 +103,7 @@
 
     @pl.when(w == 0)
     def _():
-        for i in (1, 3, 5):
+        for i in range(1, NW - 1):
             pl.semaphore_signal(
                 barrier, inc=1, device_id={"seq": lax.rem(z + NZ - 1, NZ) * NW + i}, device_id_type=MESH
             )
@@ -127,7 +128,7 @@
     own_text.start()
 
     with jax.named_scope("greeting"):
-        pl.semaphore_wait(barrier, NY - 1 + NZ - 1 + NW - 1 + 2 + jnp.minimum(w, 1) * jnp.minimum(NW - 1 - w, 1))
+        pl.semaphore_wait(barrier, NY - 1 + NZ - 1 + NW - 1 + 2 + jnp.minimum(w, 1) * jnp.minimum(NW - 1 - w, 1) * (2 - w % 2))
 
     def send_y(c):
         a, first, columns = CHUNKS[c]
@@ -151,17 +152,16 @@
 
     @pl.when(w == NW - 1)
     def _():
-        for j in range(3):
-            remote(text_ref.at[pl.ds(j * PIECE, PIECE)], relay, t_ssem.at[1], t_rsem.at[1], w_device(2 * j + 1)).start()
-        remote(
-            text_ref.at[pl.ds(3 * PIECE, PIECE)], raw.at[0, pl.ds(3 * PIECE, PIECE)], t_ssem.at[2], t_rsem.at[0], after
-        ).start()
+        for i in range(1, NW - 1):
+            remote(text_ref.at[pl.ds((i - 1) * PIECE, PIECE)], relay, t_ssem.at[1], t_rsem.at[1], w_device(i)).start()
+        rest = pl.ds(6 * PIECE, OWN_PIECE)
+        remote(text_ref.at[rest], raw.at[0, rest], t_ssem.at[2], t_rsem.at[0], after).start()
 
     def relay_prompt():
-        @pl.when((w % 2 == 1) & inner)
+        @pl.when(inner)
         def _():
             bytes_of(relay, t_ssem.at[1], t_rsem.at[1]).wait_recv()
-            piece = raw.at[0, pl.ds(pl.multiple_of((w // 2) * PIECE, 16), PIECE)]
+            piece = raw.at[0, pl.ds(pl.multiple_of((w - 1) * PIECE, 16), PIECE)]
             remote(relay, piece, t_ssem.at[2], t_rsem.at[0], up).start()
 
     def relay_near():
@@ -398,14 +398,6 @@
         packed[int(a == T), :, first : first + columns // 2] = left
         packed[int(a == T), :, first + columns // 2 : first + columns] = right
         if a == T:
-            if first == 0:
-                with jax.named_scope("prompt_arrival"):
-                    bytes_of(raw.at[0], t_ssem.at[0], t_rsem.at[0]).wait_recv()
-                with jax.named_scope("earlier_prompt"):
-                    sort_prompt(0)
-            with jax.named_scope("cross_attention"):
-                for h in heads:
-                    cross_head(h)
             return
         if first == 0:
             with jax.named_scope("near_arrival"):
@@ -430,14 +422,20 @@
             over_z(c + Z_FIRST, back_left, back_right, from_plane(c + Z_FIRST))
         if c + Z_FIRST + 1 < NC:
             plane_first(c + Z_FIRST + 1)
-        if c == 1:
+        if c == 0:
             relay_prompt()
         if c == 3:
             relay_near()
         if 0 < c <= Z_FIRST:
             use_from_plane(c - 1)
+        if c == 5:
+            bytes_of(raw.at[0], t_ssem.at[0], t_rsem.at[0]).wait_recv()
+            sort_prompt(0)
         if c >= Z_FIRST:
             use(c, dot(place_left, arrived).astype(BF16), dot(place_right, arrived).astype(BF16))
+        if c == 5:
+            for h in range(HEADS):
+                cross_head(h)
 
     @pl.when(w < NW - 1)
     def _():
@@ -445,14 +443,12 @@
 
     @pl.when(w == NW - 1)
     def _():
-        bytes_of(raw.at[0, pl.ds(0, 3 * PIECE)], t_ssem.at[1], t_rsem.at[1]).wait_send()
-
-    @pl.when(w % 2 == 1)
+        bytes_of(raw.at[0, pl.ds(0, 6 * PIECE)], t_ssem.at[1], t_rsem.at[1]).wait_send()
+        bytes_of(raw.at[0, pl.ds(0, OWN_PIECE)], t_ssem.at[2], t_rsem.at[2]).wait_send()
+
+    @pl.when(inner)
     def _():
         bytes_of(relay, t_ssem.at[2], t_rsem.at[2]).wait_send()
-
-    @pl.when(inner)
-    def _():
         bytes_of(near_relay, r_sems.at[0], r_sems.at[1]).wait_send()
 
     bytes_of(slot_send.at[pl.ds(0, NZ - 1)], s_sems.at[0], s_sems.at[1]).wait_send()

time: 77.7 us -> 77.1 us (level)
  Pallas kernels: 75.8 us -> 74.8 us
    pallas_call x1, Pallas kernels: 75.8 us -> 74.8 us  [body(): pl.pallas_call(kernel, out_shape=jax.ShapeDtypeStruct((ROWS, FEAT), BF16)...]
where the time goes in v4:
time: 77.1 us; the launch traced here: 76.4 us
  Pallas kernels  74.8 us (97%)
  local copies, waits for them, and re-layouts  1.67 us (2%)
    pallas_call x1, Pallas kernels, body(): pl.pallas_call(kernel, out_shape=jax.ShapeDtypeStruct((ROWS, FEAT), BF16)...  74.8 us
    unnamed x1, local copies, waits for them, and re-layouts  1.67 us

profile of v4, /device:TPU:1, one launch (start us, length us, event | category | flops | bytes accessed | tf_op | source)
XLA Modules:
  0.0 76.4 jit_solution(3572148882680781943)
XLA Ops:
  0.0 74.8 %shard_map.73 = bf16[128,1024]{1,0:T(8,128)(2,1)} custom-call(bf16[32,4096]{1,0:T(8,128)(2,1)} %q_ref.1, bf16[32,4096]{1,0:T(8,128)(2,1)} %k_ref.1, bf16[32,4096]{1,0:T(8,128)(2,1)} %v_ref.1, bf16[32,4096]{1,0:T(8,128)(2,1)} %t_ref.1, bf16[4800,128]{1,0:T(8,128)(2,1)} %bitcast.9, s32[1,128]{1,0:T(1,128)} %bitcast.10, s32[1,128]{1,0:T(1,128)} %bitcast.11), custom_call_target="tpu_custom_call" | custom-call | tf_op jit(solution)/shard_map/pallas_call | solution.py:491
  74.8 1.7 %copy.10 = bf16[128,1024]{1,0:T(8,128)(2,1)} copy(bf16[128,1024]{1,0:T(8,128)(2,1)} %shard_map.73) | data formatting | bytes 524288

commit v5 on v4

--- a/solution.py
+++ b/solution.py
@@ -164,7 +164,7 @@
             piece = raw.at[0, pl.ds(pl.multiple_of((w - 1) * PIECE, 16), PIECE)]
             remote(relay, piece, t_ssem.at[2], t_rsem.at[0], up).start()
 
-    def relay_near():
+    def relay_near(first, last):
         def forward(device, side):
             i = w // 2
             cols = pl.ds(pl.multiple_of((i % 2) * 512, 512), 512)
@@ -173,11 +173,11 @@
                 near_relay, kv.at[i // 2, pl.ds(2 * ROWS * side, ROWS), cols], r_sems.at[0], n_rsem.at[2 * i + side], device
             ).start()
 
-        @pl.when((w % 2 == 1) & inner)
+        @pl.when((w % 2 == 1) & (w >= first) & (w <= last))
         def _():
             forward(up, 0)
 
-        @pl.when((w % 2 == 0) & inner)
+        @pl.when((w % 2 == 0) & (w >= first) & (w <= last))
         def _():
             forward(down, 1)
 
@@ -424,8 +424,10 @@
             plane_first(c + Z_FIRST + 1)
         if c == 0:
             relay_prompt()
+        if c == 2:
+            relay_near(1, 1)
         if c == 3:
-            relay_near()
+            relay_near(2, 3)
         if 0 < c <= Z_FIRST:
             use_from_plane(c - 1)
         if c == 5:
@@ -433,6 +435,8 @@
             sort_prompt(0)
         if c >= Z_FIRST:
             use(c, dot(place_left, arrived).astype(BF16), dot(place_right, arrived).astype(BF16))
+        if c == 3:
+            relay_near(4, 6)
         if c == 5:
             for h in range(HEADS):
                 cross_head(h)

time: 77.1 us -> 77.1 us (level)
  no operation moved by 1% of the time
where the time goes in v5:
time: 77.1 us; the launch traced here: 76 us
  Pallas kernels  74.3 us (96%)
  local copies, waits for them, and re-layouts  1.67 us (2%)
    pallas_call x1, Pallas kernels, body(): pl.pallas_call(kernel, out_shape=jax.ShapeDtypeStruct((ROWS, FEAT), BF16)...  74.3 us
    unnamed x1, local copies, waits for them, and re-layouts  1.67 us

profile of v5, /device:TPU:1, one launch (start us, length us, event | category | flops | bytes accessed | tf_op | source)
XLA Modules:
  0.0 76.0 jit_solution(6147075336283752096)
XLA Ops:
  0.0 74.3 %shard_map.73 = bf16[128,1024]{1,0:T(8,128)(2,1)} custom-call(bf16[32,4096]{1,0:T(8,128)(2,1)} %q_ref.1, bf16[32,4096]{1,0:T(8,128)(2,1)} %k_ref.1, bf16[32,4096]{1,0:T(8,128)(2,1)} %v_ref.1, bf16[32,4096]{1,0:T(8,128)(2,1)} %t_ref.1, bf16[4800,128]{1,0:T(8,128)(2,1)} %bitcast.9, s32[1,128]{1,0:T(1,128)} %bitcast.10, s32[1,128]{1,0:T(1,128)} %bitcast.11), custom_call_target="tpu_custom_call" | custom-call | tf_op jit(solution)/shard_map/pallas_call | solution.py:495
  74.3 1.7 %copy.10 = bf16[128,1024]{1,0:T(8,128)(2,1)} copy(bf16[128,1024]{1,0:T(8,128)(2,1)} %shard_map.73) | data formatting | bytes 524288
